TPU v7x, 128 devices: a whole 4x4x4 slice. The times are simulated.
128 devices in a mesh: ctx: 16 (over z_hi, x, core), head: 8 (over z_lo, y).
Axes of the slice: x: 4, y: 4, z: 4 (z_hi: 2, z_lo: 2; z = z_hi * 2 + z_lo), core: 2. Of those that a mesh axis runs over, the one named last changes fastest.
Arguments:
- tokens: bfloat16 [16384, 4096], P('ctx', 'head'), may hold values from -23 to 23
- proj_weight: bfloat16 [4096, 32, 384], P(None, 'head'), may hold values from -1 to 1
- partner_shard: int32 [32, 256, 3], P('head'), may hold values from 0 to 15, all different within a row; in each aligned block of 16 rows (0 to 15, 16 to 31, ..., all dimensions but the last counted through in order) at most 6 rows name the same one
- partner_block: int32 [32, 256, 3], P('head'), may hold values from 0 to 15
Outputs:
- attended: bfloat16 [16384, 32, 128], P('ctx', 'head')
Inputs may be any that keep to these rules, and one draw needn't show every extreme that they name: `partner_shard`: the 3 entries of one row differ. For each head, within each aligned run of 16 block rows, no value is named more than 6 times, and some runs name one value exactly 6 times.
All inputs are finite; a program needn't handle non-finite values.
Results may differ from a plain program's by a relative error of at most 0.008.
Values may be sent and summed in bfloat16 or wider, within the bound.
A program may use at most 192 MiB of HBM per device.

v0:
```python
import jax
import jax.numpy as jnp
from jax import lax
from jax.sharding import PartitionSpec as P

HEAD_DIMENSION = 128
BLK = 64
GLOB = 2
RAND = 3


def padded_2(cells, sides, width):
    for axis, dim in sides:
        count = lax.axis_size(axis)
        head = lax.slice_in_dim(cells, 0, width, axis=dim)
        tail = lax.slice_in_dim(cells, cells.shape[dim] - width, cells.shape[dim], axis=dim)
        cells = jnp.concatenate(
            [
                lax.ppermute(tail, axis, [(i, (i + 1) % count) for i in range(count)]),
                cells,
                lax.ppermute(head, axis, [((i + 1) % count, i) for i in range(count)]),
            ],
            axis=dim,
        )
    return cells


def from_root(block, axis, holder):
    block = jnp.where(lax.axis_index(axis) == holder, block, jnp.zeros_like(block))
    return lax.psum(block, axis)


def combined_all(part, axis, combine):
    gathered = jax.tree.map(lambda a: lax.all_gather(a, axis), part)

    def take(source):
        return jax.tree.map(lambda a: lax.dynamic_index_in_dim(a, source, 0, False), gathered)

    return lax.fori_loop(
        1, lax.axis_size(axis), lambda source, state: combine(state, take(source)), take(0)
    )


def per_device(tokens, proj_weight, partner_shard, partner_block):
    row_count = tokens.shape[0]
    head_count = proj_weight.shape[1]
    blocks = row_count // BLK
    shard_index = lax.axis_index("ctx")
    inverse_root_scale = HEAD_DIMENSION ** (-0.5)
    packed = jnp.einsum(
        "td,dhe->the",
        lax.all_gather(tokens, "head", axis=1, tiled=True),
        proj_weight,
        preferred_element_type=jnp.float32,
    ).astype(jnp.bfloat16)
    queries = packed[..., :HEAD_DIMENSION]
    keyval = packed[..., HEAD_DIMENSION:]
    padded = padded_2(keyval, (("ctx", 0),), BLK)
    window = jnp.concatenate(
        [
            padded[0:row_count].reshape(blocks, BLK, head_count, 2 * HEAD_DIMENSION),
            padded[BLK : row_count + BLK].reshape(blocks, BLK, head_count, 2 * HEAD_DIMENSION),
            padded[2 * BLK : row_count + 2 * BLK].reshape(
                blocks, BLK, head_count, 2 * HEAD_DIMENSION
            ),
        ],
        axis=1,
    )
    global_pack = from_root(packed[: GLOB * BLK], "ctx", 0)
    global_query = global_pack[..., :HEAD_DIMENSION]
    global_keyval = global_pack[..., HEAD_DIMENSION:]
    row_total = blocks * RAND
    owners = lax.dynamic_slice_in_dim(partner_shard, shard_index * blocks, blocks, 1).reshape(
        head_count, row_total
    )
    offsets = lax.dynamic_slice_in_dim(partner_block, shard_index * blocks, blocks, 1).reshape(
        head_count, row_total
    )
    partner_index = owners * blocks + offsets
    block_rows = lax.all_gather(keyval, "ctx", axis=0, tiled=True)
    piece_blocks = block_rows.shape[0] // BLK
    piece_hot = (partner_index[..., None] == jnp.arange(piece_blocks)).astype(jnp.bfloat16)
    blocked = block_rows.reshape(piece_blocks, BLK, head_count, 2 * HEAD_DIMENSION)
    fetched = jnp.einsum(
        "hrb,bthe->hrte", piece_hot, blocked, preferred_element_type=jnp.float32
    ).astype(jnp.bfloat16)
    remote = fetched
    remote = remote.reshape(head_count, blocks, RAND * BLK, 2 * HEAD_DIMENSION)
    blocked_query_rows = queries.reshape(blocks, BLK, head_count, HEAD_DIMENSION)
    window_scores = jnp.einsum(
        "bqhd,bkhd->bhqk",
        blocked_query_rows,
        window[..., :HEAD_DIMENSION],
        preferred_element_type=jnp.float32,
    )
    global_scores = jnp.einsum(
        "bqhd,khd->bhqk",
        blocked_query_rows,
        global_keyval[..., :HEAD_DIMENSION],
        preferred_element_type=jnp.float32,
    )
    remote_scores = jnp.einsum(
        "bqhd,hbkd->bhqk",
        blocked_query_rows,
        remote[..., :HEAD_DIMENSION],
        preferred_element_type=jnp.float32,
    )
    logit_scores = (
        jnp.concatenate([window_scores, global_scores, remote_scores], axis=-1) * inverse_root_scale
    )
    softmax_weight_matrix = jax.nn.softmax(logit_scores, axis=-1).astype(jnp.bfloat16)
    width_window = 3 * BLK
    width_global = GLOB * BLK
    context = jnp.einsum(
        "bhqk,bkhd->bqhd",
        softmax_weight_matrix[..., :width_window],
        window[..., HEAD_DIMENSION:],
        preferred_element_type=jnp.float32,
    )
    context = context + jnp.einsum(
        "bhqk,khd->bqhd",
        softmax_weight_matrix[..., width_window : width_window + width_global],
        global_keyval[..., HEAD_DIMENSION:],
        preferred_element_type=jnp.float32,
    )
    context = context + jnp.einsum(
        "bhqk,hbkd->bqhd",
        softmax_weight_matrix[..., width_window + width_global :],
        remote[..., HEAD_DIMENSION:],
        preferred_element_type=jnp.float32,
    )
    sparse_attention_output = context.astype(jnp.bfloat16).reshape(
        row_count, head_count, HEAD_DIMENSION
    )
    lead_scores = (
        jnp.einsum(
            "qhd,khd->hqk",
            global_query,
            keyval[..., :HEAD_DIMENSION],
            preferred_element_type=jnp.float32,
        )
        * inverse_root_scale
    )
    maxima = jnp.max(lead_scores, axis=-1)
    exp_terms = jnp.exp(lead_scores - maxima[..., None])
    totals = jnp.sum(exp_terms, axis=-1)
    summed = jnp.einsum(
        "hqk,khd->hqd",
        exp_terms,
        keyval[..., HEAD_DIMENSION:].astype(jnp.float32),
        precision=lax.Precision.HIGHEST,
    )

    def combine(first, second):
        max_first, total_first, sum_first = first
        max_second, total_second, sum_second = second
        larger = jnp.maximum(max_first, max_second)
        factor_first = jnp.exp(max_first - larger)
        factor_second = jnp.exp(max_second - larger)
        return (
            larger,
            total_first * factor_first + total_second * factor_second,
            sum_first * factor_first[..., None] + sum_second * factor_second[..., None],
        )

    maxima, totals, summed = combined_all((maxima, totals, summed), "ctx", combine)
    global_out = jnp.transpose((summed / totals[..., None]).astype(jnp.bfloat16), (1, 0, 2))
    head_rows = jnp.where(shard_index == 0, global_out, sparse_attention_output[: GLOB * BLK])
    return jnp.concatenate([head_rows, sparse_attention_output[GLOB * BLK :]], axis=0)


def solution(mesh):
    in_specs = (
        P("ctx", "head"),
        P(None, "head", None),
        P("head", None, None),
        P("head", None, None),
    )
    out_specs = P("ctx", "head", None)
    return jax.shard_map(
        per_device, mesh=mesh, in_specs=in_specs, out_specs=out_specs, check_vma=False
    )
```

profile of v0, /device:TPU:1, one launch (start us, length us, event | category | flops | bytes accessed | tf_op | source)
XLA Modules:
  0.0 600.6 jit_solution(12266525961735290425)
XLA Ops:
  6.5 0.7 all-gather.9.cloned.1.call-update
  7.3 0.0 all-reduce.2.cloned.1.call-start
  7.3 96.9 %all-gather.9.cloned.1.call-done = bf16[1024,4096]{1,0:T(8,128)(2,1)} async-done(((bf16[1024,512]{1,0:T(8,128)(2,1)}), bf16[1024,4096]{1,0:T(8,128)(2,1)}) %all-gather.9.cloned.1.call-update) | async-done | bytes 8388624 | tf_op jit(solution)/shard_map/all_gather | solution.py:52
  104.2 18.3 %fusion.22 = bf16[1024,4,384]{2,0,1:T(8,128)(2,1)S(1)} fusion(bf16[4096,4,384]{2,1,0:T(4,128)(2,1)} %param.7, bf16[1024,4096]{1,0:T(8,128)(2,1)} %all-gather.9.cloned.1.call-done), kind=kOutput, calls=%fused_computation.29 | convolution fusion | flops 12886474752 | bytes 24117248 | tf_op jit(solution)/shard_map/td,dhe->the/dot_general | solution.py:50
  122.5 0.8 slice_select_fusion
  123.4 0.0 all-reduce.2.cloned.1.call-update
  123.4 0.0 all-gather.13.cloned.1.call-start
  123.5 137.0 %all-reduce.2.cloned.1.call-done = bf16[128,4,384]{2,0,1:T(8,128)(2,1)} async-done(((bf16[128,4,384]{2,0,1:T(8,128)(2,1)}), bf16[128,4,384]{2,0,1:T(8,128)(2,1)}) %all-reduce.2.cloned.1.call-update) | async-done | bytes 393232 | tf_op jit(solution)/shard_map/psum | solution.py:30
  260.4 1.4 multiply_reduce_fusion
  261.9 1.3 copy-done.1
  263.2 2.2 fusion.30
  265.3 0.0 all-gather.13.cloned.1.call-update
  265.3 0.0 all-gather.11.cloned.1.call-start
  265.4 1.5 slice.118
  266.9 0.0 all-gather.11.cloned.1.call-update
  266.9 1.8 fusion.56
  268.7 0.7 collective-permute-start.1
  269.4 0.8 dynamic-slice_add_fusion
  270.2 0.1 copy.40
  270.3 0.1 add.84
  270.4 1.3 slice.116
  271.7 1.4 collective-permute-done.1
  273.1 0.3 pad_maximum_fusion.2
  273.4 5.0 pad_maximum_fusion
  278.4 3.4 fusion.54
  281.9 4.1 fusion.20
  285.9 25.5 %all-gather.3 = f32[16,4,128]{2,1,0:T(4,128)S(1)} all-gather(f32[1,4,128]{2,1,0:T(4,128)S(1)} %bitcast.75), channel_id=2, replica_groups=mesh['ctx'=16,'head'=8] {'ctx'}, dimensions={0}, use_global_device_ids=true | all-gather | bytes 34816 | tf_op jit(solution)/shard_map/all_gather | solution.py:34
  311.5 0.5 fusion.31
  312.0 19.5 %all-gather.4 = f32[16,4,128]{2,1,0:T(4,128)S(1)} all-gather(f32[1,4,128]{2,1,0:T(4,128)S(1)} %bitcast.76), channel_id=3, replica_groups=mesh['ctx'=16,'head'=8] {'ctx'}, dimensions={0}, use_global_device_ids=true | all-gather | bytes 34816 | tf_op jit(solution)/shard_map/all_gather | solution.py:34
  331.4 1.3 convolution_bitcast_fusion
  332.8 0.0 all-gather.13.cloned.1.call-done
  332.8 1.0 slice.115
  333.8 19.0 %while.19 = (s32[]{:T(128)}, f32[4,128]{1,0:T(4,128)S(1)}, f32[4,128]{1,0:T(4,128)S(1)}, f32[4,128,128]{2,1,0:T(8,128)S(1)}, f32[16,4,128]{2,1,0:T(4,128)S(1)}, ...) while((s32[]{:T(128)}, f32[4,128]{1,0:T(4,128)S(1)}, ...), condition=%wide.region_4.5_spmd, body=%wide.region_3.4_spmd.sunk | while | flops 199685 | bytes 807063 | solution.py:39
  333.9 1.3 fusion.61
  335.2 1.3 fusion.61
  336.5 1.2 fusion.61
  337.8 1.3 fusion.61
  339.1 1.2 fusion.61
  340.3 1.2 fusion.61
  341.6 1.2 fusion.61
  342.8 1.2 fusion.61
  344.1 1.2 fusion.61
  345.4 1.2 fusion.61
  346.6 1.2 fusion.61
  347.9 1.2 fusion.61
  349.1 1.2 fusion.61
  350.4 1.2 fusion.61
  351.6 1.2 fusion.61
  352.9 159.2 %all-gather.11.cloned.1.call-done = bf16[16384,4,256]{2,0,1:T(8,128)(2,1)} async-done(((bf16[1024,4,256]{2,0,1:T(8,128)(2,1)}), bf16[16384,4,256]{2,0,1:T(8,128)(2,1)}) %all-gather.11.cloned.1.call-update) | async-done | bytes 33554448 | tf_op jit(solution)/shard_map/all_gather | solution.py:80
  512.1 34.4 %fusion.11 = bf16[4,48,64,256]{3,1,2,0:T(8,128)(2,1)S(1)} fusion(bf16[256,64,4,256]{3,1,0,2:T(8,128)(2,1)} %bitcast.65, s32[4,48]{1,0:T(4,128)S(1)} %add.84), kind=kOutput, calls=%fused_computation.20 | convolution fusion | flops 1613807616 | bytes 39846656 | tf_op jit(solution)/shard_map/hrb,bthe->hrte/dot_general | solution.py:84
  546.5 2.5 copy.42
  548.9 1.8 fusion.55
  550.7 4.1 fusion.18
  554.8 28.1 %fusion.57 = (f32[16,4,64]{2,1,0:T(4,128)S(1)}, f32[16,4,64,512]{3,2,1,0:T(8,128)}) fusion(f32[16,4,64,192]{3,2,1,0:T(8,128)} %fusion.18, f32[16,4,64,128]{3,2,1,0:T(8,128)S(1)} %convolution_bitcast_fusion, f32[16,4,64,192]{3,2,1,0:T(8,128)S(1)} %copy-done.5), kind=kOutput, calls=%fused_computation.71 | output fusion | flops 10486271 | bytes 16793600 | tf_op jit(solution)/shard_map/sub | solution.py:111
  582.9 4.1 divide_convert_fusion
  587.0 1.3 fusion.14
  588.2 1.6 fusion.36
  589.8 0.4 copy-done.3
  590.2 1.4 fusion.29
  591.6 0.1 slice.130
  591.7 0.1 copy.47
  591.8 0.1 bitcast_select_fusion
  592.0 0.1 pad_maximum_fusion.3
  592.1 1.8 copy.48
  (32 shorter events, 0.4 us)
Async XLA Ops:
  6.5 97.7 %all-gather.9.cloned.1.call-start = ((), (), s32[]{:S(2)}) async-start(), calls=%async_computation | async-start | bytes 9437184 | tf_op jit(solution)/shard_map/all_gather | solution.py:52
  7.3 253.2 %all-reduce.2.cloned.1.call-start = ((), (), s32[]{:S(2)}) async-start(), calls=%async_computation.1 | async-start | bytes 786432 | tf_op jit(solution)/shard_map/psum | solution.py:30
  122.5 142.9 %copy-start.4 = (bf16[1024,4,384]{2,0,1:T(8,128)(2,1)}, bf16[1024,4,384]{2,0,1:T(8,128)(2,1)S(1)}, u32[]{:S(2)}) copy-start(bf16[1024,4,384]{2,0,1:T(8,128)(2,1)S(1)} %fusion.22) | copy-start | bytes 9437188
  123.4 209.4 %all-gather.13.cloned.1.call-start = ((), (), s32[]{:S(2)}) async-start(), calls=%async_computation.3 | async-start | bytes 4456448 | tf_op jit(solution)/shard_map/all_gather | solution.py:34
  261.9 1.3 copy-start.1
  265.3 246.7 %all-gather.11.cloned.1.call-start = ((), (), s32[]{:S(2)}) async-start(), calls=%async_computation.2 | async-start | bytes 35651584 | tf_op jit(solution)/shard_map/all_gather | solution.py:80
  266.9 6.2 %copy-start = (bf16[1024,4,256]{2,0,1:T(8,128)(2,1)S(1)}, bf16[1024,4,256]{2,0,1:T(8,128)(2,1)}, u32[]{:S(2)}) copy-start(bf16[1024,4,256]{2,0,1:T(8,128)(2,1)} %slice.118) | copy-start | bytes 6291460
  268.7 3.0 collective-permute-start
  268.7 4.4 collective-permute-start.1
  281.9 29.6 %copy-start.2 = (f32[4,128,1024]{2,1,0:T(8,128)S(1)}, f32[4,128,1024]{2,1,0:T(8,128)}, u32[]{:S(2)}) copy-start(f32[4,128,1024]{2,1,0:T(8,128)} %copy-done.1) | copy-start | bytes 6291460
  550.7 4.1 copy-start.5
  588.2 2.0 copy-start.3
Sparse Core Ops, SparseCore 0:
  9.0 95.1 all-gather.8
  123.5 136.8 all-reduce.1
  265.5 57.4 all-gather.12
  325.6 186.3 all-gather.10
where the time goes:
time: 610 us; the launch traced here: 601 us
  waiting for transfers between devices  395 us (65%)
  matrix products  70 us (11%)
  other arithmetic  58.4 us (10%)
  blocking collectives  45 us (7%)
  local copies, waits for them, and re-layouts  17.1 us (3%)
  between operations  13.6 us (2%)
    all_gather x1, waiting for transfers between devices, per_device(): block_rows = lax.all_gather(keyval, 'ctx', axis=0, tiled=True)  159 us
    psum x1, waiting for transfers between devices, from_root(): return lax.psum(block, axis)  137 us
    all_gather x1, waiting for transfers between devices, per_device(): lax.all_gather(tokens, 'head', axis=1, tiled=True)  96.9 us
    all_gather x2, blocking collectives, combined_all(): gathered = jax.tree.map(lambda a: lax.all_gather(a, axis), part)  45 us
    dot_general x1, matrix products, per_device(): jnp.einsum('hrb,bthe->hrte', piece_hot, blocked, preferred_element_type=j...  34.4 us
    sub x1, other arithmetic, per_device(): jax.nn.softmax(logit_scores, axis=-1).astype(jnp.bfloat16)  28.1 us
    dot_general x1, matrix products, per_device(): jnp.einsum('td,dhe->the', lax.all_gather(tokens, 'head', axis=1, tiled=Tr...  18.3 us
    add x15, other arithmetic, combine(): sum_first * factor_first[..., None] + sum_second * factor_second[..., None]  18.3 us
  transfers between devices with their start and end apart: 6, of which 4 were waited for; matrix products, arithmetic and copies ran while one was open for 7% of the time, Pallas kernels for 0%

commit v1 on v0

v1 whole, which is shorter than its diff:
```python
import functools

import jax
import jax.numpy as jnp
from jax import lax
from jax.experimental import pallas as pl
from jax.experimental.pallas import tpu as pltpu
from jax.sharding import PartitionSpec as P

HD = 128
BLK = 64
ROWS = 1024
D = 4096
FEAT = 512
MESH = pl.DeviceIdType.MESH
CHUNKS = (256, 256, 256, 128, 128)
C2 = 1.4426950408889634 * HD**-0.5


def kernel(
    tokens, weight, part_shard, part_block, out,
    tok, stage, wv, pk, kv, q, gq, gout, gm, gl, gacc, obuf, orecv,
    wsem, lsem, ssem, rsem,
):
    ctx, hd = lax.axis_index("ctx"), lax.axis_index("head")
    zh, x, core = ctx // 8, (ctx // 2) % 4, ctx % 2
    zl, y = hd // 4, hd % 4
    g = zh * 2 + core

    def at_ctx(zh_, x_, core_):
        return (zh_ * 8 + x_ * 2 + core_, hd)

    def at_head(zl_, y_):
        return (ctx, zl_ * 4 + y_)

    up, down, far = (y + 1) % 4, (y + 3) % 4, (y + 2) % 4
    xs = [(x + d) % 4 for d in (0, 1, 2, 3)]
    zpeer = at_head(1 - zl, y)
    ypeer, mpeer = at_head(zl, up), at_head(zl, down)
    cpeer = at_ctx(zh, x, 1 - core)
    hpeer = at_ctx(1 - zh, x, core)
    dpeer = at_ctx(1 - zh, x, 1 - core)
    xpeers = [None] + [at_ctx(zh, xs[d], core) for d in (1, 2, 3)]
    gc, gz, gd = zh * 2 + 1 - core, (1 - zh) * 2 + core, (1 - zh) * 2 + 1 - core

    barrier = pltpu.get_barrier_semaphore()
    everyone = [zpeer, ypeer, mpeer, cpeer, hpeer, dpeer] + xpeers[1:]
    for peer in everyone:
        pl.semaphore_signal(barrier, inc=1, device_id=peer, device_id_type=MESH)
    pl.semaphore_wait(barrier, len(everyone))

    sems = {}
    sent = []
    local = {}

    def sem_of(key):
        return sems.setdefault(key, len(sems))

    def send(key, src, dst, peer):
        i = sem_of(key)
        copy = pltpu.make_async_remote_copy(
            src_ref=src, dst_ref=dst, send_sem=ssem.at[i], recv_sem=rsem.at[i],
            device_id=peer, device_id_type=MESH,
        )
        copy.start()
        sent.append(copy)

    def arrived(key, dst):
        i = sem_of(key)
        pltpu.make_async_remote_copy(
            src_ref=dst, dst_ref=dst, send_sem=ssem.at[i], recv_sem=rsem.at[i],
            device_id=zpeer, device_id_type=MESH,
        ).wait_recv()

    def put(key, src, dst):
        copy = pltpu.make_async_copy(src, dst, lsem.at[len(local)])
        copy.start()
        local[key] = copy

    starts = [sum(CHUNKS[:c]) for c in range(len(CHUNKS))]

    def rows_of(c):
        return pl.ds(starts[c], CHUNKS[c])

    def blocks_of(c):
        return pl.ds(starts[c] // BLK, CHUNKS[c] // BLK)

    def piece(zl_, y_, c):
        return tok.at[rows_of(c), pl.ds(pl.multiple_of((zl_ * 4 + y_) * FEAT, FEAT), FEAT)]

    def mine(c):
        return tokens.at[rows_of(c), :]

    def give_z(c):
        send(("z", c), mine(c), piece(zl, y, c), zpeer)

    def give_y(c):
        send(("yu", c), mine(c), piece(zl, y, c), ypeer)
        send(("yd", c), mine(c), piece(zl, y, c), mpeer)

    def pass_z(c):
        arrived(("z", c), piece(1 - zl, y, c))
        send(("zu", c), piece(1 - zl, y, c), piece(1 - zl, y, c), ypeer)
        send(("zd", c), piece(1 - zl, y, c), piece(1 - zl, y, c), mpeer)

    def pass_y(c):
        arrived(("yu", c), piece(zl, down, c))
        send(("fu", c), piece(zl, down, c), piece(zl, down, c), ypeer)
        arrived(("zd", c), piece(1 - zl, up, c))
        send(("fd", c), piece(1 - zl, up, c), piece(1 - zl, up, c), mpeer)

    def tokens_complete(c):
        arrived(("yd", c), piece(zl, up, c))
        arrived(("zu", c), piece(1 - zl, down, c))
        arrived(("fu", c), piece(zl, far, c))
        arrived(("fd", c), piece(1 - zl, far, c))

    def weight_copy(i):
        return pltpu.make_async_copy(
            weight.at[pl.ds(i * FEAT, FEAT)], stage.at[i % 2], wsem.at[i % 2]
        )

    def relayout(i):
        weight_copy(i).wait()
        block = jnp.swapaxes(stage[i % 2], 0, 1)
        rows = pl.ds(i * FEAT, FEAT)
        for h in range(4):
            wv[0, rows, h * HD : (h + 1) * HD] = block[h, :, :HD]
            wv[1 + h // 2, rows, (h % 2) * 256 : (h % 2 + 1) * 256] = block[h, :, HD:]
        if i + 2 < 8:
            weight_copy(i + 2).start()

    def project(c):
        def one(n, carry):
            pk[n, blocks_of(c)] = (
                jnp.dot(tok[rows_of(c), :], wv[n], preferred_element_type=jnp.float32)
                .astype(jnp.bfloat16)
                .reshape(CHUNKS[c] // BLK, BLK, 512)
            )
            return carry

        lax.fori_loop(0, 3, one, 0)

    def kv_part(h, c):
        return pk.at[1 + h // 2, blocks_of(c), :, pl.ds(pl.multiple_of((h % 2) * 256, 256), 256)]

    def q_part(h, c):
        return pk.at[0, blocks_of(c), :, pl.ds(pl.multiple_of(h * HD, HD), HD)]

    def give_x(c):
        for d in (2, 1, 3):
            send(("kv", d, c), kv_part(xs[d], c), kv.at[g * 4 + x, blocks_of(c)], xpeers[d])
        put(("kv", c), kv_part(x, c), kv.at[g * 4 + x, blocks_of(c)])
        for d in (2, 1, 3):
            send(("q", d, c), q_part(xs[d], c), q.at[x, blocks_of(c)], xpeers[d])
        put(("q", c), q_part(x, c), q.at[x, blocks_of(c)])

    def group(k, c):
        return kv.at[pl.ds(k * 4, 4), blocks_of(c)]

    def pass_x(c):
        for d in (1, 2, 3):
            arrived(("kv", d, c), kv.at[g * 4 + xs[4 - d], blocks_of(c)])
        local[("kv", c)].wait()
        send(("kz", c), group(g, c), group(g, c), hpeer)
        send(("kc", c), group(g, c), group(g, c), cpeer)
        for d in (1, 2, 3):
            arrived(("q", d, c), q.at[xs[4 - d], blocks_of(c)])
        local[("q", c)].wait()

    def pass_h(c):
        arrived(("kz", c), group(gz, c))
        send(("kd", c), group(gz, c), group(gz, c), cpeer)

    def kv_complete(c):
        arrived(("kc", c), group(gc, c))
        arrived(("kd", c), group(gd, c))

    def give_gq():
        lead = q.at[0, pl.ds(0, 2)]
        put("gq", lead, gq.at[g])
        for name, peer in (("gqc", cpeer), ("gqh", hpeer), ("gqd", dpeer)):
            send(name, lead, gq.at[g], peer)

    def take_gq():
        local["gq"].wait()
        arrived("gqc", gq.at[gc])
        arrived("gqh", gq.at[gz])
        arrived("gqd", gq.at[gd])
        gm[...] = jnp.full_like(gm, -jnp.inf)
        gl[...] = jnp.zeros_like(gl)
        gacc[...] = jnp.zeros_like(gacc)

    def lead_keys(c):
        size = CHUNKS[c]
        query = gq[0, g // 2, pl.ds(pl.multiple_of((g % 2) * 32, 32), 32), :]

        def one(k, carry):
            top, total, acc = carry
            block = kv[pl.ds(k * 4, 4), blocks_of(c)].reshape(4 * size, 256)
            s = lax.dot_general(
                query, block[:, :HD], (((1,), (1,)), ((), ())), preferred_element_type=jnp.float32
            )
            higher = jnp.maximum(top, jnp.max(s, axis=1, keepdims=True))
            p = jnp.exp2((s - higher) * C2)
            shrink = jnp.exp2((top - higher) * C2)
            total = total * shrink + jnp.sum(p, axis=1, keepdims=True)
            acc = acc * shrink + jnp.dot(
                p.astype(jnp.bfloat16), block[:, HD:], preferred_element_type=jnp.float32
            )
            return higher, total, acc

        top, total, acc = lax.fori_loop(0, 4, one, (gm[...], gl[...], gacc[...]))
        gm[...], gl[...], gacc[...] = top, total, acc

    def lead_out():
        gout[g] = (gacc[...] / gl[...]).astype(jnp.bfloat16)
        for name, peer in (("goc", cpeer), ("goh", hpeer), ("god", dpeer)):
            send(name, gout.at[g], gout.at[g], peer)

    def key_block(b):
        s, r = b // 16, b % 16
        slot = ((s // 8) * 2 + s % 2) * 4 + (s // 2) % 4
        return kv[slot, r]

    def attend(xp):
        first = (zh * 8 + xp * 2 + core) * 16

        def one(r, carry):
            b = first + r
            ids = [(b + 255) % 256, b, (b + 1) % 256, 0, 1] + [
                part_shard[j, x, b] * 16 + part_block[j, x, b] for j in range(3)
            ]
            keys = jnp.concatenate([key_block(i) for i in ids], axis=0)
            rows = pl.ds(pl.multiple_of(r * BLK, BLK), BLK)
            s = lax.dot_general(
                q[xp, r], keys[:, :HD], (((1,), (1,)), ((), ())),
                preferred_element_type=jnp.float32,
            )
            p = jnp.exp2((s - jnp.max(s, axis=1, keepdims=True)) * C2)
            total = jnp.sum(p, axis=1, keepdims=True)
            o = jnp.dot(p.astype(jnp.bfloat16), keys[:, HD:], preferred_element_type=jnp.float32)
            obuf[xp, rows, :] = (o / total).astype(jnp.bfloat16)
            return carry

        lax.fori_loop(0, 16, one, 0, unroll=2)

    last = len(CHUNKS) - 1
    weight_copy(0).start()
    weight_copy(1).start()
    give_z(0)
    give_y(0)
    give_z(1)
    put("tok", tokens, tok.at[:, pl.ds(pl.multiple_of(hd * FEAT, FEAT), FEAT)])
    for i in range(5):
        relayout(i)
    pass_z(0)
    for i in range(5, 8):
        relayout(i)
    local["tok"].wait()
    for c in range(last + 1):
        pass_y(c)
        if c + 2 <= last:
            give_z(c + 2)
        if c + 1 <= last:
            give_y(c + 1)
            pass_z(c + 1)
        if c >= 1:
            pass_x(c - 1)
            if c == 1:
                give_gq()
        if c >= 2:
            pass_h(c - 2)
        tokens_complete(c)
        project(c)
        give_x(c)
        if c >= 2:
            kv_complete(c - 2)
            if c == 2:
                take_gq()
            lead_keys(c - 2)
    pass_h(last - 1)
    pass_x(last)
    kv_complete(last - 1)
    lead_keys(last - 1)
    pass_h(last)
    kv_complete(last)
    lead_keys(last)
    lead_out()
    for d in (2, 1, 3, 0):
        attend(xs[d])
        if d == 2:
            arrived("goc", gout.at[gc])
            arrived("goh", gout.at[gz])
            arrived("god", gout.at[gd])

        @pl.when((xs[d] == 0) & (g == 0))
        def _():
            obuf[xs[d], pl.ds(0, 128), :] = gout[...].reshape(128, HD)

        if d:
            send(("o", d), obuf.at[xs[d]], orecv.at[x], xpeers[d])
        else:
            out[x] = obuf[x]
    for d in (2, 1, 3):
        arrived(("o", d), orecv.at[xs[4 - d]])
        out[xs[4 - d]] = orecv[xs[4 - d]]
    for copy in sent:
        copy.wait_send()


def per_device(tokens, proj_weight, partner_shard, partner_block):
    bf16, f32 = jnp.bfloat16, jnp.float32
    n_sems = 16 * len(CHUNKS) + 9
    out = pl.pallas_call(
        kernel,
        out_shape=jax.ShapeDtypeStruct((4, ROWS, HD), bf16),
        in_specs=[
            pl.BlockSpec(memory_space=pl.ANY),
            pl.BlockSpec(memory_space=pl.ANY),
            pl.BlockSpec(memory_space=pltpu.SMEM),
            pl.BlockSpec(memory_space=pltpu.SMEM),
        ],
        out_specs=pl.BlockSpec(memory_space=pltpu.VMEM),
        scratch_shapes=[
            pltpu.VMEM((ROWS, D), bf16),
            pltpu.VMEM((2, FEAT, 4, 384), bf16),
            pltpu.VMEM((3, D, 512), bf16),
            pltpu.VMEM((3, ROWS // BLK, BLK, 512), bf16),
            pltpu.VMEM((16, ROWS // BLK, BLK, 256), bf16),
            pltpu.VMEM((4, ROWS // BLK, BLK, HD), bf16),
            pltpu.VMEM((4, 2, BLK, HD), bf16),
            pltpu.VMEM((4, 32, HD), bf16),
            pltpu.VMEM((32, 1), f32),
            pltpu.VMEM((32, 1), f32),
            pltpu.VMEM((32, HD), f32),
            pltpu.VMEM((4, ROWS, HD), bf16),
            pltpu.VMEM((4, ROWS, HD), bf16),
            pltpu.SemaphoreType.DMA((2,)),
            pltpu.SemaphoreType.DMA((2 * len(CHUNKS) + 2,)),
            pltpu.SemaphoreType.DMA((n_sems,)),
            pltpu.SemaphoreType.DMA((n_sems,)),
        ],
        compiler_params=pltpu.CompilerParams(
            collective_id=0, has_side_effects=True, vmem_limit_bytes=58 * 2**20
        ),
    )(
        tokens,
        proj_weight,
        jnp.transpose(partner_shard, (2, 0, 1)),
        jnp.transpose(partner_block, (2, 0, 1)),
    )
    return jnp.transpose(out, (1, 0, 2))


def solution(mesh):
    in_specs = (
        P("ctx", "head"),
        P(None, "head", None),
        P("head", None, None),
        P("head", None, None),
    )
    return jax.shard_map(
        per_device, mesh=mesh, in_specs=in_specs, out_specs=P("ctx", "head", None), check_vma=False
    )
```

time: 610 us -> 133 us (0.22); the launches traced: 601 us -> 133 us
  waiting for transfers between devices: 395 us -> 0 us
  Pallas kernels: 0 us -> 130 us
  matrix products: 70 us -> 0 us
  other arithmetic: 58.4 us -> 0 us
  blocking collectives: 45 us -> 0 us
  local copies, waits for them, and re-layouts: 17.1 us -> 3.01 us
  between operations: 13.6 us -> 0.01 us
    all_gather x3 -> x0, waiting for transfers between devices: 256 us -> none  [the longest x1 159 us: per_device(): block_rows = lax.all_gather(keyval, 'ctx', axis=0, tiled=True)]
    psum x1 -> x0, waiting for transfers between devices: 137 us -> none  [from_root(): return lax.psum(block, axis)]
    pallas_call x0 -> x1, Pallas kernels: none -> 130 us  [per_device(): pl.pallas_call(kernel, out_shape=jax.ShapeDtypeStruct((4, ROWS, HD), bf16...]
    dot_general x10 -> x0, matrix products: 70 us -> none  [the longest x1 34.4 us: per_device(): jnp.einsum('hrb,bthe->hrte', piece_hot, blocked, preferred_element_type=j...]
    all_gather x2 -> x0, blocking collectives: 45 us -> none  [combined_all(): gathered = jax.tree.map(lambda a: lax.all_gather(a, axis), part)]
    sub x1 -> x0, other arithmetic: 28.1 us -> none  [per_device(): jax.nn.softmax(logit_scores, axis=-1).astype(jnp.bfloat16)]
    add x31 -> x0, other arithmetic: 19.4 us -> none  [the longest x15 18.3 us: combine(): sum_first * factor_first[..., None] + sum_second * factor_second[..., None]]
    slice x9 -> x0, local copies, waits for them, and re-layouts: 10 us -> none  [the longest x1 3.45 us: per_device(): window[..., HEAD_DIMENSION:]]
  transfers between devices with their start and end apart: 6 -> 0, of which waited for: 4 -> 0; matrix products, arithmetic and copies ran while one was open for 7% -> 0% of each run, Pallas kernels for 0% -> 0%
where the time goes in v1:
time: 133 us
  Pallas kernels  130 us (98%)
  local copies, waits for them, and re-layouts  3.01 us (2%)
    pallas_call x1, Pallas kernels, per_device(): pl.pallas_call(kernel, out_shape=jax.ShapeDtypeStruct((4, ROWS, HD), bf16...  130 us
    transpose x1, local copies, waits for them, and re-layouts, per_device(): return jnp.transpose(out, (1, 0, 2))  3.01 us

profile of v1, /device:TPU:1, one launch (start us, length us, event | category | flops | bytes accessed | tf_op | source)
XLA Modules:
  0.0 133.0 jit_solution(82799020526570075)
XLA Ops:
  0.0 130.0 %shard_map.46 = bf16[4,1024,128]{2,1,0:T(8,128)(2,1)} custom-call(bf16[1024,512]{1,0:T(8,128)(2,1)} %tokens.1, bf16[4096,4,384]{2,1,0:T(4,128)(2,1)} %weight.1, s32[3,4,256]{2,1,0:T(4,128)} %bitcast.4, s32[3,4,256]{2,1,0:T(4,128)} %bitcast.5), custom_call_target="tpu_custom_call" | custom-call | tf_op jit(solution)/shard_map/pallas_call | solution.py:315
  130.0 3.0 %copy.5 = bf16[1024,4,128]{2,1,0:T(4,128)(2,1)} copy(bf16[1024,4,128]{2,0,1:T(8,128)(2,1)} %bitcast.3) | data formatting | bytes 2097152 | tf_op jit(solution)/shard_map/transpose | solution.py:353

commit v2 on v1

--- a/solution.py
+++ b/solution.py
@@ -14,12 +14,14 @@
 FEAT = 512
 MESH = pl.DeviceIdType.MESH
 CHUNKS = (256, 256, 256, 128, 128)
+DIRECT = (len(CHUNKS) - 1,)
+ZUP = 2
 C2 = 1.4426950408889634 * HD**-0.5
 
 
 def kernel(
     tokens, weight, part_shard, part_block, out,
-    tok, stage, wv, pk, kv, q, gq, gout, gm, gl, gacc, obuf, orecv,
+    tok, stage, wv, pk, kv, q, gq, gout, gm, gl, gacc, obuf, orecv, ids,
     wsem, lsem, ssem, rsem,
 ):
     ctx, hd = lax.axis_index("ctx"), lax.axis_index("head")
@@ -41,10 +43,19 @@
     hpeer = at_ctx(1 - zh, x, core)
     dpeer = at_ctx(1 - zh, x, 1 - core)
     xpeers = [None] + [at_ctx(zh, xs[d], core) for d in (1, 2, 3)]
+    hpeers = [hpeer] + [at_ctx(1 - zh, xs[d], core) for d in (1, 2, 3)]
     gc, gz, gd = zh * 2 + 1 - core, (1 - zh) * 2 + core, (1 - zh) * 2 + 1 - core
 
+    def weight_copy(i):
+        return pltpu.make_async_copy(
+            weight.at[pl.ds(i * FEAT, FEAT)], stage.at[i % 2], wsem.at[i % 2]
+        )
+
+    weight_copy(0).start()
+    weight_copy(1).start()
+
     barrier = pltpu.get_barrier_semaphore()
-    everyone = [zpeer, ypeer, mpeer, cpeer, hpeer, dpeer] + xpeers[1:]
+    everyone = [zpeer, ypeer, mpeer, cpeer, dpeer] + xpeers[1:] + hpeers
     for peer in everyone:
         pl.semaphore_signal(barrier, inc=1, device_id=peer, device_id_type=MESH)
     pl.semaphore_wait(barrier, len(everyone))
@@ -77,6 +88,7 @@
         copy.start()
         local[key] = copy
 
+    last = len(CHUNKS) - 1
     starts = [sum(CHUNKS[:c]) for c in range(len(CHUNKS))]
 
     def rows_of(c):
@@ -114,11 +126,6 @@
         arrived(("zu", c), piece(1 - zl, down, c))
         arrived(("fu", c), piece(zl, far, c))
         arrived(("fd", c), piece(1 - zl, far, c))
-
-    def weight_copy(i):
-        return pltpu.make_async_copy(
-            weight.at[pl.ds(i * FEAT, FEAT)], stage.at[i % 2], wsem.at[i % 2]
-        )
 
     def relayout(i):
         weight_copy(i).wait()
@@ -149,7 +156,11 @@
 
     def give_x(c):
         for d in (2, 1, 3):
+            if c in DIRECT:
+                send(("kh", d), kv_part(xs[d], c), kv.at[g * 4 + x, blocks_of(c)], hpeers[d])
             send(("kv", d, c), kv_part(xs[d], c), kv.at[g * 4 + x, blocks_of(c)], xpeers[d])
+        if c in DIRECT:
+            send(("kh", 0), kv_part(x, c), kv.at[g * 4 + x, blocks_of(c)], hpeer)
         put(("kv", c), kv_part(x, c), kv.at[g * 4 + x, blocks_of(c)])
         for d in (2, 1, 3):
             send(("q", d, c), q_part(xs[d], c), q.at[x, blocks_of(c)], xpeers[d])
@@ -162,14 +173,19 @@
         for d in (1, 2, 3):
             arrived(("kv", d, c), kv.at[g * 4 + xs[4 - d], blocks_of(c)])
         local[("kv", c)].wait()
-        send(("kz", c), group(g, c), group(g, c), hpeer)
+        if c not in DIRECT:
+            send(("kz", c), group(g, c), group(g, c), hpeer)
         send(("kc", c), group(g, c), group(g, c), cpeer)
         for d in (1, 2, 3):
             arrived(("q", d, c), q.at[xs[4 - d], blocks_of(c)])
         local[("q", c)].wait()
 
     def pass_h(c):
-        arrived(("kz", c), group(gz, c))
+        if c not in DIRECT:
+            arrived(("kz", c), group(gz, c))
+        else:
+            for d in (0, 1, 2, 3):
+                arrived(("kh", d), kv.at[gz * 4 + xs[(4 - d) % 4], blocks_of(c)])
         send(("kd", c), group(gz, c), group(gz, c), cpeer)
 
     def kv_complete(c):
@@ -218,49 +234,55 @@
         for name, peer in (("goc", cpeer), ("goh", hpeer), ("god", dpeer)):
             send(name, gout.at[g], gout.at[g], peer)
 
-    def key_block(b):
-        s, r = b // 16, b % 16
-        slot = ((s // 8) * 2 + s % 2) * 4 + (s // 2) % 4
-        return kv[slot, r]
-
-    def attend(xp):
-        first = (zh * 8 + xp * 2 + core) * 16
-
+    def slot_of(s):
+        return (s & 8) | ((s & 1) << 2) | ((s >> 1) & 3)
+
+    def place_of(b):
+        return (slot_of(b >> 4) << 4) | (b & 15)
+
+    def prepare(d):
         def one(r, carry):
-            b = first + r
-            ids = [(b + 255) % 256, b, (b + 1) % 256, 0, 1] + [
-                part_shard[j, x, b] * 16 + part_block[j, x, b] for j in range(3)
-            ]
-            keys = jnp.concatenate([key_block(i) for i in ids], axis=0)
-            rows = pl.ds(pl.multiple_of(r * BLK, BLK), BLK)
-            s = lax.dot_general(
-                q[xp, r], keys[:, :HD], (((1,), (1,)), ((), ())),
-                preferred_element_type=jnp.float32,
-            )
-            p = jnp.exp2((s - jnp.max(s, axis=1, keepdims=True)) * C2)
-            total = jnp.sum(p, axis=1, keepdims=True)
-            o = jnp.dot(p.astype(jnp.bfloat16), keys[:, HD:], preferred_element_type=jnp.float32)
-            obuf[xp, rows, :] = (o / total).astype(jnp.bfloat16)
+            b = ((zh * 8 + xs[d] * 2 + core) << 4) + r
+            n = (d * 16 + r) * 6
+            for t, k in enumerate(((b + 255) & 255, b, (b + 1) & 255)):
+                ids[n + t] = place_of(k)
+            for j in range(3):
+                ids[n + 3 + j] = (slot_of(part_shard[j, x, b]) << 4) + part_block[j, x, b]
             return carry
 
-        lax.fori_loop(0, 16, one, 0, unroll=2)
-
-    last = len(CHUNKS) - 1
-    weight_copy(0).start()
-    weight_copy(1).start()
+        lax.fori_loop(0, 16, one, 0)
+
+    def key_block(i):
+        return kv[i >> 4, i & 15]
+
+    def attend(d, r):
+        places = [ids[(d * 16 + r) * 6 + t] for t in range(6)]
+        places = places[:3] + [0, 1] + places[3:]
+        keys = jnp.concatenate([key_block(i) for i in places], axis=0)
+        s = lax.dot_general(
+            q[xs[d], r], keys[:, :HD], (((1,), (1,)), ((), ())), preferred_element_type=jnp.float32
+        )
+        p = jnp.exp2((s - jnp.max(s, axis=1, keepdims=True)) * C2).astype(jnp.bfloat16)
+        values = jnp.concatenate([keys[:, HD:], jnp.ones((512, HD), jnp.bfloat16)], axis=1)
+        o = jnp.dot(p, values, preferred_element_type=jnp.float32)
+        obuf[xs[d], r * BLK : (r + 1) * BLK, :] = (o[:, :HD] / o[:, HD:]).astype(jnp.bfloat16)
+
     give_z(0)
     give_y(0)
-    give_z(1)
+    for c in range(1, ZUP):
+        give_z(c)
     put("tok", tokens, tok.at[:, pl.ds(pl.multiple_of(hd * FEAT, FEAT), FEAT)])
     for i in range(5):
         relayout(i)
     pass_z(0)
     for i in range(5, 8):
         relayout(i)
+    for d in range(4):
+        prepare(d)
     local["tok"].wait()
     for c in range(last + 1):
         pass_y(c)
-        if c + 2 <= last:
+        if ZUP <= c + 2 <= last:
             give_z(c + 2)
         if c + 1 <= last:
             give_y(c + 1)
@@ -275,43 +297,51 @@
         project(c)
         give_x(c)
         if c >= 2:
-            kv_complete(c - 2)
             if c == 2:
+                kv_complete(0)
                 take_gq()
-            lead_keys(c - 2)
+            else:
+                kv_complete(c - 2)
+            if c < last:
+                lead_keys(c - 2)
     pass_h(last - 1)
     pass_x(last)
     kv_complete(last - 1)
-    lead_keys(last - 1)
     pass_h(last)
     kv_complete(last)
-    lead_keys(last)
-    lead_out()
-    for d in (2, 1, 3, 0):
-        attend(xs[d])
-        if d == 2:
+    half = ROWS // 2
+    for step, (d, part) in enumerate(((2, 1), (1, 1), (3, 1), (2, 0), (1, 0), (3, 0), (0, 1), (0, 0))):
+        if step == 3:
+            for c in range(last - 2, last + 1):
+                lead_keys(c)
+            lead_out()
+        for r in range(part * 8, part * 8 + 8):
+            attend(d, r)
+        rows = pl.ds(part * half, half)
+        if step == 3:
             arrived("goc", gout.at[gc])
             arrived("goh", gout.at[gz])
             arrived("god", gout.at[gd])
-
-        @pl.when((xs[d] == 0) & (g == 0))
-        def _():
-            obuf[xs[d], pl.ds(0, 128), :] = gout[...].reshape(128, HD)
-
+        if part == 0:
+            @pl.when((xs[d] == 0) & (g == 0))
+            def _():
+                obuf[xs[d], pl.ds(0, 128), :] = gout[...].reshape(128, HD)
         if d:
-            send(("o", d), obuf.at[xs[d]], orecv.at[x], xpeers[d])
+            send(("o", d, part), obuf.at[xs[d], rows], orecv.at[x, rows], xpeers[d])
         else:
-            out[x] = obuf[x]
-    for d in (2, 1, 3):
-        arrived(("o", d), orecv.at[xs[4 - d]])
-        out[xs[4 - d]] = orecv[xs[4 - d]]
+            out[x, rows, :] = obuf[x, rows, :]
+    for part in (1, 0):
+        rows = pl.ds(part * half, half)
+        for d in (2, 1, 3):
+            arrived(("o", d, part), orecv.at[xs[4 - d], rows])
+            out[xs[4 - d], rows, :] = orecv[xs[4 - d], rows, :]
     for copy in sent:
         copy.wait_send()
 
 
 def per_device(tokens, proj_weight, partner_shard, partner_block):
     bf16, f32 = jnp.bfloat16, jnp.float32
-    n_sems = 16 * len(CHUNKS) + 9
+    n_sems = 16 * len(CHUNKS) + 15
     out = pl.pallas_call(
         kernel,
         out_shape=jax.ShapeDtypeStruct((4, ROWS, HD), bf16),
@@ -336,6 +366,7 @@
             pltpu.VMEM((32, HD), f32),
             pltpu.VMEM((4, ROWS, HD), bf16),
             pltpu.VMEM((4, ROWS, HD), bf16),
+            pltpu.SMEM((64 * 6,), jnp.int32),
             pltpu.SemaphoreType.DMA((2,)),
             pltpu.SemaphoreType.DMA((2 * len(CHUNKS) + 2,)),
             pltpu.SemaphoreType.DMA((n_sems,)),

time: 133 us -> 125 us (0.940)
  Pallas kernels: 130 us -> 121 us
    pallas_call x1, Pallas kernels: 130 us -> 121 us  [per_device(): pl.pallas_call(kernel, out_shape=jax.ShapeDtypeStruct((4, ROWS, HD), bf16...]
where the time goes in v2:
time: 125 us; the launch traced here: 124 us
  Pallas kernels  121 us (97%)
  local copies, waits for them, and re-layouts  3.01 us (2%)
    pallas_call x1, Pallas kernels, per_device(): pl.pallas_call(kernel, out_shape=jax.ShapeDtypeStruct((4, ROWS, HD), bf16...  121 us
    transpose x1, local copies, waits for them, and re-layouts, per_device(): return jnp.transpose(out, (1, 0, 2))  3.01 us

profile of v2, /device:TPU:1, one launch (start us, length us, event | category | flops | bytes accessed | tf_op | source)
XLA Modules:
  0.0 124.3 jit_solution(15671510140461406676)
XLA Ops:
  0.0 121.3 %shard_map.46 = bf16[4,1024,128]{2,1,0:T(8,128)(2,1)} custom-call(bf16[1024,512]{1,0:T(8,128)(2,1)} %tokens.1, bf16[4096,4,384]{2,1,0:T(4,128)(2,1)} %weight.1, s32[3,4,256]{2,1,0:T(4,128)} %bitcast.4, s32[3,4,256]{2,1,0:T(4,128)} %bitcast.5), custom_call_target="tpu_custom_call" | custom-call | tf_op jit(solution)/shard_map/pallas_call | solution.py:345
  121.3 3.0 %copy.5 = bf16[1024,4,128]{2,1,0:T(4,128)(2,1)} copy(bf16[1024,4,128]{2,0,1:T(8,128)(2,1)} %bitcast.3) | data formatting | bytes 2097152 | tf_op jit(solution)/shard_map/transpose | solution.py:384

commit v3 on v2

--- a/solution.py
+++ b/solution.py
@@ -16,12 +16,13 @@
 CHUNKS = (256, 256, 256, 128, 128)
 DIRECT = (len(CHUNKS) - 1,)
 ZUP = 2
+PARTS = 4
 C2 = 1.4426950408889634 * HD**-0.5
 
 
 def kernel(
     tokens, weight, part_shard, part_block, out,
-    tok, stage, wv, pk, kv, q, gq, gout, gm, gl, gacc, obuf, orecv, ids,
+    tok, stage, wv, pk, kv, q, gq, gout, gm, gl, gacc, obuf, ids,
     wsem, lsem, ssem, rsem,
 ):
     ctx, hd = lax.axis_index("ctx"), lax.axis_index("head")
@@ -208,12 +209,12 @@
         gacc[...] = jnp.zeros_like(gacc)
 
     def lead_keys(c):
-        size = CHUNKS[c]
-        query = gq[0, g // 2, pl.ds(pl.multiple_of((g % 2) * 32, 32), 32), :]
+        size = 2 * CHUNKS[c]
+        query = gq[0].reshape(128, HD)
 
         def one(k, carry):
             top, total, acc = carry
-            block = kv[pl.ds(k * 4, 4), blocks_of(c)].reshape(4 * size, 256)
+            block = kv[pl.ds(g * 4 + k * 2, 2), blocks_of(c)].reshape(size, 256)
             s = lax.dot_general(
                 query, block[:, :HD], (((1,), (1,)), ((), ())), preferred_element_type=jnp.float32
             )
@@ -226,11 +227,13 @@
             )
             return higher, total, acc
 
-        top, total, acc = lax.fori_loop(0, 4, one, (gm[...], gl[...], gacc[...]))
+        top, total, acc = lax.fori_loop(0, 2, one, (gm[...], gl[...], gacc[...]))
         gm[...], gl[...], gacc[...] = top, total, acc
 
     def lead_out():
-        gout[g] = (gacc[...] / gl[...]).astype(jnp.bfloat16)
+        lane = lax.broadcasted_iota(jnp.int32, (128, HD), 1)
+        gout[g, 0] = gacc[...]
+        gout[g, 1] = jnp.where(lane < 64, gm[...], gl[...])
         for name, peer in (("goc", cpeer), ("goh", hpeer), ("god", dpeer)):
             send(name, gout.at[g], gout.at[g], peer)
 
@@ -267,81 +270,94 @@
         o = jnp.dot(p, values, preferred_element_type=jnp.float32)
         obuf[xs[d], r * BLK : (r + 1) * BLK, :] = (o[:, :HD] / o[:, HD:]).astype(jnp.bfloat16)
 
+    def lead_rows(d):
+        if d == 2:
+            arrived("goc", gout.at[gc])
+            arrived("goh", gout.at[gz])
+            arrived("god", gout.at[gd])
+
+        @pl.when((xs[d] == 0) & (g == 0))
+        def _():
+            tops = [gout[k, 1, :, 0:1] for k in range(4)]
+            totals = [gout[k, 1, :, 64:65] for k in range(4)]
+            top = functools.reduce(jnp.maximum, tops)
+            shrink = [jnp.exp2((t - top) * C2) for t in tops]
+            total = sum(t * f for t, f in zip(totals, shrink))
+            acc = sum(gout[k, 0] * shrink[k] for k in range(4))
+            obuf[xs[d], pl.ds(0, 128), :] = (acc / total).astype(jnp.bfloat16)
+
     give_z(0)
     give_y(0)
     for c in range(1, ZUP):
         give_z(c)
     put("tok", tokens, tok.at[:, pl.ds(pl.multiple_of(hd * FEAT, FEAT), FEAT)])
-    for i in range(5):
+    for i in range(4):
         relayout(i)
     pass_z(0)
-    for i in range(5, 8):
+    for i in range(4, 6):
         relayout(i)
+    pass_y(0)
+    give_z(2)
+    give_y(1)
+    for i in range(6, 8):
+        relayout(i)
+    pass_z(1)
     for d in range(4):
         prepare(d)
     local["tok"].wait()
     for c in range(last + 1):
-        pass_y(c)
-        if ZUP <= c + 2 <= last:
-            give_z(c + 2)
-        if c + 1 <= last:
-            give_y(c + 1)
-            pass_z(c + 1)
+        if c:
+            pass_y(c)
+            if c + 2 <= last:
+                give_z(c + 2)
+            if c + 1 <= last:
+                give_y(c + 1)
+                pass_z(c + 1)
         if c >= 1:
             pass_x(c - 1)
             if c == 1:
                 give_gq()
         if c >= 2:
             pass_h(c - 2)
+            if c == 2:
+                take_gq()
+            lead_keys(c - 2)
         tokens_complete(c)
         project(c)
         give_x(c)
-        if c >= 2:
-            if c == 2:
-                kv_complete(0)
-                take_gq()
-            else:
-                kv_complete(c - 2)
-            if c < last:
-                lead_keys(c - 2)
     pass_h(last - 1)
+    lead_keys(last - 1)
     pass_x(last)
-    kv_complete(last - 1)
+    lead_keys(last)
     pass_h(last)
-    kv_complete(last)
-    half = ROWS // 2
-    for step, (d, part) in enumerate(((2, 1), (1, 1), (3, 1), (2, 0), (1, 0), (3, 0), (0, 1), (0, 0))):
-        if step == 3:
-            for c in range(last - 2, last + 1):
-                lead_keys(c)
-            lead_out()
-        for r in range(part * 8, part * 8 + 8):
-            attend(d, r)
-        rows = pl.ds(part * half, half)
-        if step == 3:
-            arrived("goc", gout.at[gc])
-            arrived("goh", gout.at[gz])
-            arrived("god", gout.at[gd])
-        if part == 0:
-            @pl.when((xs[d] == 0) & (g == 0))
-            def _():
-                obuf[xs[d], pl.ds(0, 128), :] = gout[...].reshape(128, HD)
-        if d:
-            send(("o", d, part), obuf.at[xs[d], rows], orecv.at[x, rows], xpeers[d])
-        else:
-            out[x, rows, :] = obuf[x, rows, :]
-    for part in (1, 0):
-        rows = pl.ds(part * half, half)
+    for c in range(last + 1):
+        kv_complete(c)
+    lead_out()
+    size = ROWS // PARTS
+    for part in range(PARTS - 1, -1, -1):
+        rows = pl.ds(part * size, size)
         for d in (2, 1, 3):
-            arrived(("o", d, part), orecv.at[xs[4 - d], rows])
-            out[xs[4 - d], rows, :] = orecv[xs[4 - d], rows, :]
+            for r in range(part * size // BLK, (part + 1) * size // BLK):
+                attend(d, r)
+            if part == 0:
+                lead_rows(d)
+            send(("o", d, part), obuf.at[xs[d], rows], out.at[x, rows], xpeers[d])
+    for r in range(16):
+        attend(0, r)
+    lead_rows(0)
+    put("out", obuf.at[x], out.at[x])
+    for part in range(PARTS - 1, -1, -1):
+        rows = pl.ds(part * size, size)
+        for d in (2, 1, 3):
+            arrived(("o", d, part), out.at[xs[4 - d], rows])
+    local["out"].wait()
     for copy in sent:
         copy.wait_send()
 
 
 def per_device(tokens, proj_weight, partner_shard, partner_block):
     bf16, f32 = jnp.bfloat16, jnp.float32
-    n_sems = 16 * len(CHUNKS) + 15
+    n_sems = 16 * len(CHUNKS) + 9 + 3 * PARTS
     out = pl.pallas_call(
         kernel,
         out_shape=jax.ShapeDtypeStruct((4, ROWS, HD), bf16),
@@ -351,7 +367,7 @@
             pl.BlockSpec(memory_space=pltpu.SMEM),
             pl.BlockSpec(memory_space=pltpu.SMEM),
         ],
-        out_specs=pl.BlockSpec(memory_space=pltpu.VMEM),
+        out_specs=pl.BlockSpec(memory_space=pl.ANY),
         scratch_shapes=[
             pltpu.VMEM((ROWS, D), bf16),
             pltpu.VMEM((2, FEAT, 4, 384), bf16),
@@ -360,15 +376,14 @@
             pltpu.VMEM((16, ROWS // BLK, BLK, 256), bf16),
             pltpu.VMEM((4, ROWS // BLK, BLK, HD), bf16),
             pltpu.VMEM((4, 2, BLK, HD), bf16),
-            pltpu.VMEM((4, 32, HD), bf16),
-            pltpu.VMEM((32, 1), f32),
-            pltpu.VMEM((32, 1), f32),
-            pltpu.VMEM((32, HD), f32),
-            pltpu.VMEM((4, ROWS, HD), bf16),
+            pltpu.VMEM((4, 2, 128, HD), f32),
+            pltpu.VMEM((128, 1), f32),
+            pltpu.VMEM((128, 1), f32),
+            pltpu.VMEM((128, HD), f32),
             pltpu.VMEM((4, ROWS, HD), bf16),
             pltpu.SMEM((64 * 6,), jnp.int32),
             pltpu.SemaphoreType.DMA((2,)),
-            pltpu.SemaphoreType.DMA((2 * len(CHUNKS) + 2,)),
+            pltpu.SemaphoreType.DMA((2 * len(CHUNKS) + 3,)),
             pltpu.SemaphoreType.DMA((n_sems,)),
             pltpu.SemaphoreType.DMA((n_sems,)),
         ],

time: 125 us -> 121 us (0.968)
  Pallas kernels: 121 us -> 118 us
    pallas_call x1, Pallas kernels: 121 us -> 118 us  [per_device(): pl.pallas_call(kernel, out_shape=jax.ShapeDtypeStruct((4, ROWS, HD), bf16...]
where the time goes in v3:
time: 121 us
  Pallas kernels  118 us (98%)
  local copies, waits for them, and re-layouts  3.01 us (2%)
    pallas_call x1, Pallas kernels, per_device(): pl.pallas_call(kernel, out_shape=jax.ShapeDtypeStruct((4, ROWS, HD), bf16...  118 us
    transpose x1, local copies, waits for them, and re-layouts, per_device(): return jnp.transpose(out, (1, 0, 2))  3.01 us

profile of v3, /device:TPU:1, one launch (start us, length us, event | category | flops | bytes accessed | tf_op | source)
XLA Modules:
  0.0 120.9 jit_solution(14683729040486379881)
XLA Ops:
  0.0 117.9 %shard_map.46 = bf16[4,1024,128]{2,1,0:T(8,128)(2,1)} custom-call(bf16[1024,512]{1,0:T(8,128)(2,1)} %tokens.1, bf16[4096,4,384]{2,1,0:T(4,128)(2,1)} %weight.1, s32[3,4,256]{2,1,0:T(4,128)} %bitcast.4, s32[3,4,256]{2,1,0:T(4,128)} %bitcast.5), custom_call_target="tpu_custom_call" | custom-call | tf_op jit(solution)/shard_map/pallas_call | solution.py:361
  117.9 3.0 %copy.5 = bf16[1024,4,128]{2,1,0:T(4,128)(2,1)} copy(bf16[1024,4,128]{2,0,1:T(8,128)(2,1)} %bitcast.3) | data formatting | bytes 2097152 | tf_op jit(solution)/shard_map/transpose | solution.py:399

commit v4 on v3

--- a/solution.py
+++ b/solution.py
@@ -13,9 +13,8 @@
 D = 4096
 FEAT = 512
 MESH = pl.DeviceIdType.MESH
-CHUNKS = (256, 256, 256, 128, 128)
+CHUNKS = (128, 256, 256, 256, 128)
 DIRECT = (len(CHUNKS) - 1,)
-ZUP = 2
 PARTS = 4
 C2 = 1.4426950408889634 * HD**-0.5
 
@@ -286,37 +285,57 @@
             acc = sum(gout[k, 0] * shrink[k] for k in range(4))
             obuf[xs[d], pl.ds(0, 128), :] = (acc / total).astype(jnp.bfloat16)
 
-    give_z(0)
+    def far_half(k):
+        rows = pl.ds(k * CHUNKS[0] // 2, CHUNKS[0] // 2)
+        return lambda y_: tok.at[rows, pl.ds(pl.multiple_of((zl * 4 + y_) * FEAT, FEAT), FEAT)]
+
+    def over_z(k, y_):
+        send(("b", k), piece(zl, y_, 0), piece(zl, y_, 0), zpeer)
+
+    send(("b", 0), mine(0), piece(zl, y, 0), zpeer)
     give_y(0)
-    for c in range(1, ZUP):
-        give_z(c)
+    give_z(1)
+    give_y(1)
     put("tok", tokens, tok.at[:, pl.ds(pl.multiple_of(hd * FEAT, FEAT), FEAT)])
-    for i in range(4):
+    for i in range(3):
         relayout(i)
-    pass_z(0)
-    for i in range(4, 6):
+    arrived(("yu", 0), piece(zl, down, 0))
+    send(("fu", 0), far_half(0)(down), far_half(0)(down), ypeer)
+    over_z(1, down)
+    arrived(("yd", 0), piece(zl, up, 0))
+    send(("fd", 0), far_half(1)(up), far_half(1)(up), mpeer)
+    over_z(2, up)
+    for i in range(3, 6):
         relayout(i)
-    pass_y(0)
+    pass_z(1)
+    arrived(("fu", 0), far_half(0)(far))
+    arrived(("fd", 0), far_half(1)(far))
+    over_z(3, far)
     give_z(2)
-    give_y(1)
     for i in range(6, 8):
         relayout(i)
-    pass_z(1)
     for d in range(4):
         prepare(d)
     local["tok"].wait()
-    for c in range(last + 1):
-        if c:
+    pass_y(1)
+    give_y(2)
+    for k, y_ in enumerate((y, down, up, far)):
+        arrived(("b", k), piece(1 - zl, y_, 0))
+    project(0)
+    give_x(0)
+    pass_z(2)
+    give_z(3)
+    for c in range(1, last + 1):
+        if c >= 2:
             pass_y(c)
             if c + 2 <= last:
                 give_z(c + 2)
             if c + 1 <= last:
                 give_y(c + 1)
                 pass_z(c + 1)
-        if c >= 1:
-            pass_x(c - 1)
-            if c == 1:
-                give_gq()
+        pass_x(c - 1)
+        if c == 1:
+            give_gq()
         if c >= 2:
             pass_h(c - 2)
             if c == 2:
@@ -357,7 +376,7 @@
 
 def per_device(tokens, proj_weight, partner_shard, partner_block):
     bf16, f32 = jnp.bfloat16, jnp.float32
-    n_sems = 16 * len(CHUNKS) + 9 + 3 * PARTS
+    n_sems = 16 * len(CHUNKS) + 10 + 3 * PARTS
     out = pl.pallas_call(
         kernel,
         out_shape=jax.ShapeDtypeStruct((4, ROWS, HD), bf16),

time: 121 us -> 117 us (0.967); the launches traced: 121 us -> 116 us
  Pallas kernels: 118 us -> 113 us
    pallas_call x1, Pallas kernels: 118 us -> 113 us  [per_device(): pl.pallas_call(kernel, out_shape=jax.ShapeDtypeStruct((4, ROWS, HD), bf16...]
where the time goes in v4:
time: 117 us; the launch traced here: 116 us
  Pallas kernels  113 us (97%)
  local copies, waits for them, and re-layouts  3.01 us (3%)
    pallas_call x1, Pallas kernels, per_device(): pl.pallas_call(kernel, out_shape=jax.ShapeDtypeStruct((4, ROWS, HD), bf16...  113 us
    transpose x1, local copies, waits for them, and re-layouts, per_device(): return jnp.transpose(out, (1, 0, 2))  3.01 us

profile of v4, /device:TPU:1, one launch (start us, length us, event | category | flops | bytes accessed | tf_op | source)
XLA Modules:
  0.0 115.6 jit_solution(11524585821554584525)
XLA Ops:
  0.0 112.6 %shard_map.46 = bf16[4,1024,128]{2,1,0:T(8,128)(2,1)} custom-call(bf16[1024,512]{1,0:T(8,128)(2,1)} %tokens.1, bf16[4096,4,384]{2,1,0:T(4,128)(2,1)} %weight.1, s32[3,4,256]{2,1,0:T(4,128)} %bitcast.4, s32[3,4,256]{2,1,0:T(4,128)} %bitcast.5), custom_call_target="tpu_custom_call" | custom-call | tf_op jit(solution)/shard_map/pallas_call | solution.py:380
  112.6 3.0 %copy.5 = bf16[1024,4,128]{2,1,0:T(4,128)(2,1)} copy(bf16[1024,4,128]{2,0,1:T(8,128)(2,1)} %bitcast.3) | data formatting | bytes 2097152 | tf_op jit(solution)/shard_map/transpose | solution.py:418

commit v5 on v4

--- a/solution.py
+++ b/solution.py
@@ -13,7 +13,7 @@
 D = 4096
 FEAT = 512
 MESH = pl.DeviceIdType.MESH
-CHUNKS = (128, 256, 256, 256, 128)
+CHUNKS = (128, 320, 256, 192, 128)
 DIRECT = (len(CHUNKS) - 1,)
 PARTS = 4
 C2 = 1.4426950408889634 * HD**-0.5

time: 117 us -> 112 us (0.957)
  Pallas kernels: 113 us -> 109 us
    pallas_call x1, Pallas kernels: 113 us -> 109 us  [per_device(): pl.pallas_call(kernel, out_shape=jax.ShapeDtypeStruct((4, ROWS, HD), bf16...]
where the time goes in v5:
time: 112 us
  Pallas kernels  109 us (97%)
  local copies, waits for them, and re-layouts  3.01 us (3%)
    pallas_call x1, Pallas kernels, per_device(): pl.pallas_call(kernel, out_shape=jax.ShapeDtypeStruct((4, ROWS, HD), bf16...  109 us
    transpose x1, local copies, waits for them, and re-layouts, per_device(): return jnp.transpose(out, (1, 0, 2))  3.01 us

profile of v5, /device:TPU:1, one launch (start us, length us, event | category | flops | bytes accessed | tf_op | source)
XLA Modules:
  0.0 111.6 jit_solution(2091367990976818166)
XLA Ops:
  0.0 108.6 %shard_map.46 = bf16[4,1024,128]{2,1,0:T(8,128)(2,1)} custom-call(bf16[1024,512]{1,0:T(8,128)(2,1)} %tokens.1, bf16[4096,4,384]{2,1,0:T(4,128)(2,1)} %weight.1, s32[3,4,256]{2,1,0:T(4,128)} %bitcast.4, s32[3,4,256]{2,1,0:T(4,128)} %bitcast.5), custom_call_target="tpu_custom_call" | custom-call | tf_op jit(solution)/shard_map/pallas_call | solution.py:380
  108.6 3.0 %copy.5 = bf16[1024,4,128]{2,1,0:T(4,128)(2,1)} copy(bf16[1024,4,128]{2,0,1:T(8,128)(2,1)} %bitcast.3) | data formatting | bytes 2097152 | tf_op jit(solution)/shard_map/transpose | solution.py:418

commit v6 on v5

--- a/solution.py
+++ b/solution.py
@@ -344,8 +344,8 @@
         tokens_complete(c)
         project(c)
         give_x(c)
+    lead_keys(last - 1)
     pass_h(last - 1)
-    lead_keys(last - 1)
     pass_x(last)
     lead_keys(last)
     pass_h(last)

time: 112 us -> 111 us (level)
  no operation moved by 1% of the time
where the time goes in v6:
time: 111 us
  Pallas kernels  108 us (97%)
  local copies, waits for them, and re-layouts  3.01 us (3%)
    pallas_call x1, Pallas kernels, per_device(): pl.pallas_call(kernel, out_shape=jax.ShapeDtypeStruct((4, ROWS, HD), bf16...  108 us
    transpose x1, local copies, waits for them, and re-layouts, per_device(): return jnp.transpose(out, (1, 0, 2))  3.01 us

profile of v6, /device:TPU:1, one launch (start us, length us, event | category | flops | bytes accessed | tf_op | source)
XLA Modules:
  0.0 110.7 jit_solution(2123879548459649858)
XLA Ops:
  0.0 107.7 %shard_map.46 = bf16[4,1024,128]{2,1,0:T(8,128)(2,1)} custom-call(bf16[1024,512]{1,0:T(8,128)(2,1)} %tokens.1, bf16[4096,4,384]{2,1,0:T(4,128)(2,1)} %weight.1, s32[3,4,256]{2,1,0:T(4,128)} %bitcast.4, s32[3,4,256]{2,1,0:T(4,128)} %bitcast.5), custom_call_target="tpu_custom_call" | custom-call | tf_op jit(solution)/shard_map/pallas_call | solution.py:380
  107.7 3.0 %copy.5 = bf16[1024,4,128]{2,1,0:T(4,128)(2,1)} copy(bf16[1024,4,128]{2,0,1:T(8,128)(2,1)} %bitcast.3) | data formatting | bytes 2097152 | tf_op jit(solution)/shard_map/transpose | solution.py:418
